TPU v7x, 32 devices: a whole 2x2x4 slice. The times are simulated.
32 devices in a mesh: dp: 4 (over x, core), ctx: 8 (over z, y).
Axes of the slice: x: 2, y: 2, z: 4, core: 2. Of those that a mesh axis runs over, the one named last changes fastest.
Arguments:
- queries: bfloat16 [4, 16, 24576], P('dp', 'ctx'), may hold values from -6 to 6
- grad_out: bfloat16 [4, 16, 16384], P('dp', 'ctx'), may hold values from -64 to 64
- latent: bfloat16 [4, 1024, 576], P('dp', 'ctx'), may hold values from -6 to 6
- latent_up: bfloat16 [512, 32768], P(None, 'ctx'), may hold values from -0.25 to 0.25
- query_start: int32 [4], P('dp'), may hold values from 2 to 1008
- key_lengths: int32 [4], P('dp'), may hold values from 18 to 1024, as said below
Outputs:
- grad_queries: float32 [4, 16, 24576], P('dp', 'ctx')
- grad_latent: float32 [4, 1024, 576], P('dp', 'ctx')
- grad_latent_up: float32 [512, 32768], P('dp', 'ctx')
Inputs may be any that keep to these rules, and one draw needn't show every extreme that they name: key_lengths[g] is at most query_start[g] + 16.
All inputs are finite; a program needn't handle non-finite values.
Results may differ from a plain program's by a relative error of at most 0.015.
Values may be sent and summed in bfloat16 or wider, within the bound.
A program may use at most 128 MiB of HBM per device.

v0:
```python
import math

import jax
import jax.numpy as jnp
from jax import lax
from jax.sharding import PartitionSpec as P

DN = 128
DR = 64
DV = 128
C = 512


MSCALE = 0.1 * math.log(40.0) + 1.0
NEG_FILL = -1e30


def local(queries, grad_out, latent, latent_up, query_start, key_lengths):
    score_scale = MSCALE * MSCALE / math.sqrt(DN + DR)
    regrouped, grads_in = (
        lax.all_to_all(queries, "ctx", split_axis=2, concat_axis=1, tiled=True),
        lax.all_to_all(grad_out, "ctx", split_axis=2, concat_axis=1, tiled=True),
    )
    query_rows = regrouped.shape[1]
    head_count = latent_up.shape[1] // (DN + DV)
    row_count = query_rows * head_count
    query_all = regrouped[0].reshape(query_rows, head_count, DN + DR)
    grad_heads = grads_in[0].reshape(query_rows, head_count, DV)
    weights_all = latent_up.reshape(C, head_count, DN + DV)
    q_nope = query_all[:, :, :DN]
    q_rope = query_all[:, :, DN:]
    w_key = weights_all[:, :, :DN]
    w_value = weights_all[:, :, DN:]
    q_latent = jnp.einsum("qhd,chd->qhc", q_nope, w_key, preferred_element_type=jnp.float32).astype(
        jnp.bfloat16
    )
    g_latent = jnp.einsum(
        "qhd,chd->qhc", grad_heads, w_value, preferred_element_type=jnp.float32
    ).astype(jnp.bfloat16)
    q_full = jnp.concatenate([q_latent, q_rope], axis=2).reshape(row_count, C + DR)
    g_rows = g_latent.reshape(row_count, C)
    all_keys = lax.all_gather(latent, "ctx", axis=1, tiled=True)[0]
    key_count = all_keys.shape[0]
    slice_start = query_start[0]
    window_low = slice_start + query_rows - key_lengths[0]
    row_pos = slice_start + jnp.arange(row_count, dtype=jnp.int32) // head_count
    key_pos = jnp.arange(key_count, dtype=jnp.int32)
    raw = (
        jnp.einsum("rc,kc->rk", q_full, all_keys, preferred_element_type=jnp.float32) * score_scale
    )
    visible = (key_pos[None, :] >= window_low) & (key_pos[None, :] <= row_pos[:, None])
    masked = jnp.where(visible, raw, NEG_FILL)
    row_peak = jnp.max(masked, axis=1, keepdims=True)
    weights = jnp.where(visible, jnp.exp(masked - row_peak), 0.0)
    attn = weights / jnp.sum(weights, axis=1, keepdims=True)
    probs_low = attn.astype(jnp.bfloat16)
    o_latent = jnp.dot(probs_low, all_keys[:, :C], preferred_element_type=jnp.float32)
    grad_probs = jnp.einsum(
        "rc,kc->rk", g_rows, all_keys[:, :C], preferred_element_type=jnp.float32
    )
    row_dot = jnp.sum(probs_low.astype(jnp.float32) * grad_probs, axis=1, keepdims=True)
    grad_scores = (score_scale * attn * (grad_probs - row_dot)).astype(jnp.bfloat16)
    key_side = jnp.einsum("rk,rc->kc", grad_scores, q_full, preferred_element_type=jnp.float32)
    value_side = jnp.einsum("rk,rc->kc", probs_low, g_rows, preferred_element_type=jnp.float32)
    key_grad = lax.psum_scatter(
        (key_side + jnp.pad(value_side, ((0, 0), (0, DR)))).astype(jnp.bfloat16),
        "ctx",
        scatter_dimension=0,
        tiled=True,
    ).astype(jnp.float32)
    query_grad = jnp.dot(grad_scores, all_keys, preferred_element_type=jnp.float32)
    grad_lat = query_grad[:, :C].astype(jnp.bfloat16).reshape(query_rows, head_count, C)
    grad_nope = jnp.einsum("qhc,chd->qhd", grad_lat, w_key, preferred_element_type=jnp.float32)
    grad_rope = query_grad[:, C:].reshape(query_rows, head_count, DR)
    grad_query = jnp.concatenate([grad_nope, grad_rope], axis=2).reshape(
        1, query_rows, head_count * (DN + DR)
    )
    grad_queries = lax.all_to_all(
        grad_query.astype(jnp.bfloat16), "ctx", split_axis=1, concat_axis=2, tiled=True
    ).astype(grad_query.dtype)
    o_low = o_latent.astype(jnp.bfloat16).reshape(query_rows, head_count, C)
    key_weight = jnp.einsum("qhc,qhd->chd", grad_lat, q_nope, preferred_element_type=jnp.float32)
    value_weight = jnp.einsum("qhc,qhd->chd", o_low, grad_heads, preferred_element_type=jnp.float32)
    grad_weights = lax.psum_scatter(
        jnp.concatenate([key_weight, value_weight], axis=2)
        .reshape(C // lax.axis_size("dp") * lax.axis_size("dp"), head_count * (DN + DV))
        .astype(jnp.bfloat16),
        "dp",
        scatter_dimension=0,
        tiled=True,
    ).astype(jnp.float32)
    return (grad_queries, key_grad[None], grad_weights)


def solution(mesh):
    return jax.shard_map(
        local,
        mesh=mesh,
        in_specs=(
            P("dp", "ctx", None),
            P("dp", "ctx", None),
            P("dp", "ctx", None),
            P(None, "ctx"),
            P("dp"),
            P("dp"),
        ),
        out_specs=(P("dp", "ctx", None), P("dp", "ctx", None), P("dp", "ctx")),
        check_vma=False,
    )
```

profile of v0, /device:TPU:0, one launch (start us, length us, event | category | flops | bytes accessed | tf_op | source)
XLA Modules:
  0.0 508.4 jit_solution(14226959686363969866)
XLA Ops:
  7.9 15.3 %copy.85 = bf16[1,2,16384]{1,0,2:T(2,128)(2,1)} copy(bf16[1,2,16384]{2,1,0:T(2,128)(2,1)} %param.7) | data formatting | bytes 131072 | tf_op args[1]
  23.7 90.8 %reduce.1 = bf16[16384,2]{1,0:T(8,128)(2,1)} reduce(bf16[16384,1,2]{2,1,0:T(2,128)(2,1)} %bitcast.71, bf16[]{:T(256)} %broadcast.49), dimensions={1}, to_apply=%bitcast.48.reduce_sub_computation | reduce | bytes 131074
  114.5 7.8 %reshape.92 = bf16[8,2,2048]{2,1,0:T(2,128)(2,1)} reshape(bf16[16384,2]{1,0:T(8,128)(2,1)} %reduce.1) | data formatting | bytes 131072
  122.3 7.3 %all-to-all-start.1 = ((bf16[8,2,2048]{2,1,0:T(2,128)(2,1)}), bf16[8,2,2048]{2,1,0:T(2,128)(2,1)S(1)}, u32[]{:S(2)}, u32[]{:S(2)}) async-start(bf16[8,2,2048]{2,1,0:T(2,128)(2,1)} %reshape.92), calls=%async_computation.1 | async-start | bytes 131072 | tf_op jit(solution)/shard_map/all_to_all | solution.py:22
  130.9 19.4 %copy.78 = bf16[1,2,24576]{1,0,2:T(2,128)(2,1)} copy(bf16[1,2,24576]{2,1,0:T(2,128)(2,1)S(1)} %copy-done.2) | data formatting | bytes 196608 | tf_op args[0]
  150.2 135.0 %reduce = bf16[24576,2]{1,0:T(8,128)(2,1)} reduce(bf16[24576,1,2]{2,1,0:T(2,128)(2,1)} %bitcast.70, bf16[]{:T(256)} %broadcast.49), dimensions={1}, to_apply=%bitcast.50.reduce_sub_computation | reduce | bytes 196610
  285.2 11.9 %reshape.94 = bf16[8,2,3072]{2,1,0:T(2,128)(2,1)} reshape(bf16[24576,2]{1,0:T(8,128)(2,1)} %reduce) | data formatting | bytes 196608
  297.1 6.5 %copy.76 = bf16[512,4096]{0,1:T(8,128)(2,1)} copy(bf16[512,4096]{1,0:T(8,128)(2,1)} %param.9) | data formatting | bytes 8388608 | tf_op args[3]
  303.6 6.0 %all-to-all-start = ((bf16[8,2,3072]{2,1,0:T(2,128)(2,1)}), bf16[8,2,3072]{2,1,0:T(2,128)(2,1)S(1)}, u32[]{:S(2)}, u32[]{:S(2)}) async-start(bf16[8,2,3072]{2,1,0:T(2,128)(2,1)} %reshape.94), calls=%async_computation | async-start | bytes 196608 | tf_op jit(solution)/shard_map/all_to_all | solution.py:21
  309.9 10.9 %reshape.93 = bf16[16384,1,2]{2,1,0:T(2,128)(2,1)} reshape(bf16[8,2,2048]{2,1,0:T(2,128)(2,1)S(1)} %all-to-all-done.1) | data formatting | bytes 131072
  320.8 15.3 %copy.86 = bf16[1,2,16384]{2,1,0:T(2,128)(2,1)S(1)} copy(bf16[1,2,16384]{1,0,2:T(2,128)(2,1)} %bitcast.72) | data formatting | bytes 131072 | tf_op jit(solution)/shard_map/all_to_all | solution.py:22
  336.3 2.0 fusion.13
  338.5 16.0 %reshape.95 = bf16[24576,1,2]{2,1,0:T(2,128)(2,1)} reshape(bf16[8,2,3072]{2,1,0:T(2,128)(2,1)S(1)} %all-to-all-done) | data formatting | bytes 196608
  354.4 23.3 %copy.79 = bf16[1,2,24576]{2,1,0:T(2,128)(2,1)S(1)} copy(bf16[1,2,24576]{1,0,2:T(2,128)(2,1)} %bitcast.69) | data formatting | bytes 196608 | tf_op jit(solution)/shard_map/all_to_all | solution.py:21
  378.0 2.0 fusion.16
  380.2 2.0 fusion.46
  387.2 1.8 convolution_convert_fusion
  391.7 2.3 pad_maximum_fusion
  394.0 6.4 %copy.100 = bf16[512,4096]{1,0:T(8,128)(2,1)} copy(bf16[512,4096]{0,1:T(8,128)(2,1)} %bitcast.76) | data formatting | bytes 8388608 | tf_op jit(solution)/shard_map/convert_element_type | solution.py:87
  400.6 2.3 fusion.22
  404.4 13.1 %all_to_all.39 = bf16[8,2,3072]{2,1,0:T(2,128)(2,1)S(1)} all-to-all(bf16[8,2,3072]{2,1,0:T(2,128)(2,1)S(1)} %reshape.96), channel_id=1, replica_groups=mesh['dp'=4,'ctx'=8] {'ctx'}, dimensions={0} | all-to-all | bytes 196608 | tf_op jit(solution)/shard_map/all_to_all | solution.py:78
  418.7 34.4 %reduce-scatter.7.cloned.1.call-done = bf16[128,576]{1,0:T(8,128)(2,1)} async-done(((bf16[1024,576]{1,0:T(8,128)(2,1)}), bf16[128,576]{1,0:T(8,128)(2,1)}) %reduce-scatter.7.cloned.1.call-update) | async-done | bytes 147472
  454.9 44.2 %reduce-scatter.5.cloned.1.call-done = bf16[128,4096]{1,0:T(8,128)(2,1)} async-done(((bf16[512,4096]{1,0:T(8,128)(2,1)}), bf16[128,4096]{1,0:T(8,128)(2,1)}) %reduce-scatter.5.cloned.1.call-update) | async-done | bytes 1048592 | tf_op jit(solution)/shard_map/reduce_scatter | solution.py:84
  499.1 2.8 convert_element_type.85
  (55 shorter events, 14.6 us)
Async XLA Ops:
  7.2 373.0 %all-gather.2.cloned.1.call-start = ((), (), s32[]{:S(2)}) async-start(), calls=%async_computation.5 | async-start | bytes 1327104 | tf_op jit(solution)/shard_map/all_gather | solution.py:42
  114.5 16.4 %copy-start.2 = (bf16[1,2,24576]{2,1,0:T(2,128)(2,1)S(1)}, bf16[1,2,24576]{2,1,0:T(2,128)(2,1)}, u32[]{:S(2)}) copy-start(bf16[1,2,24576]{2,1,0:T(2,128)(2,1)} %param.6) | copy-start | bytes 294916
  122.3 181.4 %all-to-all-start.1 = ((bf16[8,2,2048]{2,1,0:T(2,128)(2,1)}), bf16[8,2,2048]{2,1,0:T(2,128)(2,1)S(1)}, u32[]{:S(2)}, u32[]{:S(2)}) async-start(bf16[8,2,2048]{2,1,0:T(2,128)(2,1)} %reshape.92), calls=%async_computation.1 | async-start | bytes 131072 | tf_op jit(solution)/shard_map/all_to_all | solution.py:22
  303.6 34.8 %all-to-all-start = ((bf16[8,2,3072]{2,1,0:T(2,128)(2,1)}), bf16[8,2,3072]{2,1,0:T(2,128)(2,1)S(1)}, u32[]{:S(2)}, u32[]{:S(2)}) async-start(bf16[8,2,3072]{2,1,0:T(2,128)(2,1)} %reshape.94), calls=%async_computation | async-start | bytes 196608 | tf_op jit(solution)/shard_map/all_to_all | solution.py:21
  309.6 143.5 %reduce-scatter.7.cloned.1.call-start = ((), (), s32[]{:S(2)}) async-start(), calls=%async_computation.7 | async-start | bytes 1474560
  382.7 1.3 copy-start
  387.2 112.0 %reduce-scatter.5.cloned.1.call-start = ((), (), s32[]{:S(2)}) async-start(), calls=%async_computation.6 | async-start | bytes 5242880 | tf_op jit(solution)/shard_map/reduce_scatter | solution.py:84
  389.0 1.3 copy-start.1
Sparse Core Ops, SparseCore 0:
  10.0 43.6 all-gather.1
  387.3 65.7 reduce-scatter.6
  455.6 43.4 reduce-scatter.4
where the time goes:
time: 511 us; the launch traced here: 508 us
  other arithmetic  234 us (46%)
  local copies, waits for them, and re-layouts  139 us (27%)
  waiting for transfers between devices  79.4 us (16%)
  between operations  15.3 us (3%)
  matrix products  14.1 us (3%)
  starting transfers between devices  13.6 us (3%)
  blocking collectives  13.1 us (3%)
    unnamed x3, other arithmetic  227 us
    unnamed x21, local copies, waits for them, and re-layouts  91.7 us
    reduce_scatter x1, waiting for transfers between devices, local(): lax.psum_scatter(jnp.concatenate([key_weight, value_weight], axis=2).resh...  44.2 us
    unnamed x4, waiting for transfers between devices  35.1 us
    all_to_all x2, local copies, waits for them, and re-layouts, local(): lax.all_to_all(queries, 'ctx', split_axis=2, concat_axis=1, tiled=True)  23.4 us
    all_to_all x2, local copies, waits for them, and re-layouts, local(): lax.all_to_all(grad_out, 'ctx', split_axis=2, concat_axis=1, tiled=True)  15.4 us
    all_to_all x1, blocking collectives, local(): lax.all_to_all(grad_query.astype(jnp.bfloat16), 'ctx', split_axis=1, conc...  13.1 us
  transfers between devices with their start and end apart: 5, of which 2 were waited for; matrix products, arithmetic and copies ran while one was open for 74% of the time, Pallas kernels for 0%

commit v1 on v0

v1 whole, which is shorter than its diff:
```python
import functools
import math

import jax
import jax.numpy as jnp
from jax import lax
from jax.experimental import pallas as pl
from jax.experimental.pallas import tpu as pltpu
from jax.sharding import PartitionSpec as P

DN = 128
DR = 64
DV = 128
C = 512

MSCALE = 0.1 * math.log(40.0) + 1.0
NEG_FILL = -1e30
SCALE = MSCALE * MSCALE / math.sqrt(DN + DR)
CHUNKS = 2
MESH = pl.DeviceIdType.MESH
F32 = jnp.float32
BF16 = jnp.bfloat16


def dot(a, b, da, db):
    return lax.dot_general(a, b, (((da,), (db,)), ((), ())), preferred_element_type=F32)


def grid_of(n):
    inner = 1
    while (2 * inner) ** 2 <= n and n % (2 * inner) == 0:
        inner *= 2
    return n // inner, inner


def kernel(
    n_dp, n_ctx, start_ref, length_ref, q_ref, g_ref, lat_ref, w_hbm,
    gq_out, gl_out, gw_out,
    w, q_recv, g_recv, q_rows, g_rows, nope, gout, q_full, g_lat, keys,
    probs_all, grads_all, o_low, grad_lat, rope_grad,
    wg, core_recv, x_send, x_recv,
    kt_send, kt_recv, kt_own, z_send, z_recv,
    gq_rows, gq_send, gq_recv,
    w_sem, q_ss, q_rs, g_ss, g_rs, az_ss, az_rs, ay_ss, ay_rs,
    c_ss, c_rs, x_ss, x_rs, ky_ss, ky_rs, kz_ss, kz_rs, o_ss, o_rs,
):
    nz, ny = grid_of(n_ctx)
    ncore = 2 if n_dp % 2 == 0 else 1
    nx = n_dp // ncore
    dp = lax.axis_index("dp")
    me = lax.axis_index("ctx")
    z, y = me // ny, me % ny
    x, core = dp // ncore, dp % ncore
    other = (core + 1) % ncore
    rq = q_ref.shape[1]
    nq = rq * n_ctx
    wq = q_ref.shape[2] // n_ctx
    wv = g_ref.shape[2] // n_ctx
    heads = wv // DV
    rows = heads * nq
    lb = lat_ref.shape[1]
    nk = lb * n_ctx
    cr = C // n_dp

    def ctx_dev(i):
        return (dp, i)

    def dp_dev(xi, ci):
        return (xi * ncore + ci, me)

    def copy(src, dst, ss, rs, dev):
        return pltpu.make_async_remote_copy(
            src_ref=src, dst_ref=dst, send_sem=ss, recv_sem=rs, device_id=dev, device_id_type=MESH
        )

    w_copy = pltpu.make_async_copy(w_hbm, w, w_sem)
    w_copy.start()

    barrier = pltpu.get_barrier_semaphore()
    peers = [ctx_dev((me + d) % n_ctx) for d in range(1, n_ctx)]
    peers += [dp_dev((x + d) % nx, core) for d in range(1, nx)]
    if ncore > 1:
        peers.append(dp_dev(x, other))
    for dev in peers:
        pl.semaphore_signal(barrier, inc=1, device_id=dev, device_id_type=MESH)
    pl.semaphore_wait(barrier, len(peers))

    sends = []
    for d in range(1, n_ctx):
        j = (me + d) % n_ctx
        at = pl.ds(pl.multiple_of(j * wq, 128), wq)
        sends.append(copy(q_ref.at[0, :, at], q_recv.at[me], q_ss.at[d - 1], q_rs.at[d - 1], ctx_dev(j)))
        at = pl.ds(pl.multiple_of(j * wv, 128), wv)
        sends.append(copy(g_ref.at[0, :, at], g_recv.at[me], g_ss.at[d - 1], g_rs.at[d - 1], ctx_dev(j)))
    for s in sends:
        s.start()
    for d in range(1, nz):
        to = ((z + d) % nz) * ny + y
        s = copy(lat_ref.at[0], keys.at[me], az_ss.at[d - 1], az_rs.at[d - 1], ctx_dev(to))
        s.start()
        sends.append(s)

    def forward(k, src, block):
        for d in range(1, ny):
            to = z * ny + (y + d) % ny
            i = (d - 1) * nz + k
            s = copy(src, keys.at[block], ay_ss.at[i], ay_rs.at[i], ctx_dev(to))
            s.start()
            sends.append(s)

    forward(0, lat_ref.at[0], me)
    keys[me] = lat_ref[0]
    q_recv[me] = q_ref[0, :, pl.ds(pl.multiple_of(me * wq, 128), wq)]
    g_recv[me] = g_ref[0, :, pl.ds(pl.multiple_of(me * wv, 128), wv)]

    for d in range(1, n_ctx):
        j = (me - d + n_ctx) % n_ctx
        copy(q_recv.at[j], q_recv.at[j], q_ss.at[d - 1], q_rs.at[d - 1], ctx_dev(j)).wait_recv()
        copy(g_recv.at[j], g_recv.at[j], g_ss.at[d - 1], g_rs.at[d - 1], ctx_dev(j)).wait_recv()
    for j in range(n_ctx):
        q_rows[rq * j : rq * (j + 1), :] = q_recv[j].astype(F32)
        g_rows[rq * j : rq * (j + 1), :] = g_recv[j].astype(F32)
    w_copy.wait()

    def latents(h):
        at = slice(h * nq, (h + 1) * nq)
        qh = q_rows[:, h * (DN + DR) : (h + 1) * (DN + DR)].astype(BF16)
        gh = g_rows[:, h * DV : (h + 1) * DV].astype(BF16)
        nope[h] = qh[:, :DN]
        gout[h] = gh
        col = h * (DN + DV)
        q_full[at, :C] = dot(qh[:, :DN], w[:, col : col + DN], 1, 1).astype(BF16)
        q_full[at, C:] = qh[:, DN:]
        g_lat[at, :] = dot(gh, w[:, col + DN : col + DN + DV], 1, 1).astype(BF16)

    per = -(-heads // nz)
    for h in range(heads):
        latents(h)
        d = (h + 1) // per
        if (h + 1) % per == 0 and d < nz:
            block = ((z - d + nz) % nz) * ny + y
            copy(keys.at[block], keys.at[block], az_ss.at[d - 1], az_rs.at[d - 1], ctx_dev(block)).wait_recv()
            forward(d, keys.at[block], block)
    for d in range(heads // per + 1 if heads // per < nz else nz, nz):
        block = ((z - d + nz) % nz) * ny + y
        copy(keys.at[block], keys.at[block], az_ss.at[d - 1], az_rs.at[d - 1], ctx_dev(block)).wait_recv()
        forward(d, keys.at[block], block)
    for k in range(nz):
        for d in range(1, ny):
            block = ((z - k + nz) % nz) * ny + (y - d + ny) % ny
            i = (d - 1) * nz + k
            copy(keys.at[block], keys.at[block], ay_ss.at[i], ay_rs.at[i], ctx_dev(block)).wait_recv()

    start = start_ref[0]
    low = start + nq - length_ref[0]
    hc = heads // CHUNKS
    rc = hc * nq
    cw = hc * (DN + DV)

    def attend(c):
        at = slice(c * rc, (c + 1) * rc)
        all_keys = keys[...].reshape(nk, C + DR)
        raw = dot(q_full[at, :], all_keys, 1, 1) * SCALE
        key_pos = lax.broadcasted_iota(jnp.int32, (rc, nk), 1)
        row_pos = start + lax.broadcasted_iota(jnp.int32, (rc, nk), 0) % nq
        visible = (key_pos >= low) & (key_pos <= row_pos)
        masked = jnp.where(visible, raw, NEG_FILL)
        peak = jnp.max(masked, axis=1, keepdims=True)
        weights = jnp.where(visible, jnp.exp(masked - peak), 0.0)
        attn = weights * (1.0 / jnp.sum(weights, axis=1, keepdims=True))
        probs_low = attn.astype(BF16)
        probs_all[at, :] = probs_low
        o_low[at, :] = dot(probs_low, all_keys[:, :C], 1, 0).astype(BF16)
        grad_probs = dot(g_lat[at, :], all_keys[:, :C], 1, 1)
        row_dot = jnp.sum(probs_low.astype(F32) * grad_probs, axis=1, keepdims=True)
        grads = (SCALE * attn * (grad_probs - row_dot)).astype(BF16)
        grads_all[at, :] = grads
        query_grad = dot(grads, all_keys, 1, 0)
        grad_lat[at, :] = query_grad[:, :C].astype(BF16)
        rope_grad[at, :] = query_grad[:, C:]

    def weight_grads(c):
        for i in range(hc):
            h = c * hc + i
            at = slice(h * nq, (h + 1) * nq)
            col = i * (DN + DV)
            key_w = dot(grad_lat[at, :], nope[h], 0, 0).astype(BF16)
            value_w = dot(o_low[at, :], gout[h], 0, 0).astype(BF16)
            for b in range(n_dp):
                part = slice(b * cr, (b + 1) * cr)
                wg[c, b % ncore, b // ncore, :, col : col + DN] = key_w[part]
                wg[c, b % ncore, b // ncore, :, col + DN : col + DN + DV] = value_w[part]
        if ncore > 1:
            s = copy(wg.at[c, other], core_recv.at[c], c_ss.at[c], c_rs.at[c], dp_dev(x, other))
            s.start()
            sends.append(s)

    def core_sum(c, xi):
        own = wg[c, core, xi].astype(F32)
        if ncore > 1:
            own = own + core_recv[c, xi].astype(F32)
        return own

    def across_x(c):
        if ncore > 1:
            copy(core_recv.at[c], core_recv.at[c], c_ss.at[c], c_rs.at[c], dp_dev(x, other)).wait_recv()
        for d in range(1, nx):
            xi = (x + d) % nx
            i = c * (nx - 1) + d - 1
            x_send[i] = core_sum(c, xi).astype(BF16)
            s = copy(x_send.at[i], x_recv.at[i], x_ss.at[i], x_rs.at[i], dp_dev(xi, core))
            s.start()
            sends.append(s)

    def key_block(block):
        cols = pl.ds(pl.multiple_of(block * lb, lb), lb)
        key_side = dot(grads_all[:, cols], q_full[...], 0, 0)
        value_side = dot(probs_all[:, cols], g_lat[...], 0, 0)
        return key_side[:, :C] + value_side, key_side[:, C:]

    for c in range(CHUNKS):
        attend(c)
        if c:
            across_x(c - 1)
        weight_grads(c)

    for k in range(nz):
        for d in range(1, ny):
            yi = (y + d) % ny
            block = ((z + k + 1) % nz) * ny + yi
            i = (d - 1) * nz + k
            left, right = key_block(block)
            kt_send[i, :, :C] = left.astype(BF16)
            kt_send[i, :, C:] = right.astype(BF16)
            s = copy(kt_send.at[i], kt_recv.at[i], ky_ss.at[i], ky_rs.at[i], ctx_dev(z * ny + yi))
            s.start()
            sends.append(s)
    across_x(CHUNKS - 1)
    for k in range(nz):
        left, right = key_block(((z + k + 1) % nz) * ny + y)
        kt_own[k, :, :C] = left
        kt_own[k, :, C:] = right

    def inner_sum(k):
        total = kt_own[k]
        for d in range(1, ny):
            i = (d - 1) * nz + k
            copy(kt_recv.at[i], kt_recv.at[i], ky_ss.at[i], ky_rs.at[i], ctx_dev(me)).wait_recv()
            total = total + kt_recv[i].astype(F32)
        return total

    for k in range(nz - 1):
        z_send[k] = inner_sum(k).astype(BF16)
        to = ((z + k + 1) % nz) * ny + y
        s = copy(z_send.at[k], z_recv.at[k], kz_ss.at[k], kz_rs.at[k], ctx_dev(to))
        s.start()
        sends.append(s)

    for h in range(heads):
        at = slice(h * nq, (h + 1) * nq)
        col = h * (DN + DV)
        to = h * (DN + DR)
        gq_rows[:, to : to + DN] = dot(grad_lat[at, :], w[:, col : col + DN], 1, 0)
        gq_rows[:, to + DN : to + DN + DR] = rope_grad[at, :]
    for j in range(n_ctx):
        gq_send[j] = gq_rows[rq * j : rq * (j + 1), :]
    for d in range(1, n_ctx):
        j = (me + d) % n_ctx
        s = copy(gq_send.at[j], gq_recv.at[me], o_ss.at[d - 1], o_rs.at[d - 1], ctx_dev(j))
        s.start()
        sends.append(s)
    gq_recv[me] = gq_send[me]

    total = inner_sum(nz - 1)
    for k in range(nz - 1):
        copy(z_recv.at[k], z_recv.at[k], kz_ss.at[k], kz_rs.at[k], ctx_dev(me)).wait_recv()
        total = total + z_recv[k].astype(F32)
    gl_out[0] = total

    for d in range(1, n_ctx):
        j = (me - d + n_ctx) % n_ctx
        copy(gq_recv.at[j], gq_recv.at[j], o_ss.at[d - 1], o_rs.at[d - 1], ctx_dev(j)).wait_recv()
    for j in range(n_ctx):
        gq_out[0, :, j * wq : (j + 1) * wq] = gq_recv[j]

    for c in range(CHUNKS):
        part = core_sum(c, x)
        for d in range(1, nx):
            i = c * (nx - 1) + d - 1
            copy(x_recv.at[i], x_recv.at[i], x_ss.at[i], x_rs.at[i], dp_dev(x, core)).wait_recv()
            part = part + x_recv[i].astype(F32)
        gw_out[:, c * cw : (c + 1) * cw] = part
    for s in sends:
        s.wait_send()


def local(n_dp, n_ctx, queries, grad_out, latent, latent_up, query_start, key_lengths):
    nz, ny = grid_of(n_ctx)
    ncore = 2 if n_dp % 2 == 0 else 1
    nx = n_dp // ncore
    rq = queries.shape[1]
    nq = rq * n_ctx
    wq = queries.shape[2] // n_ctx
    wv = grad_out.shape[2] // n_ctx
    heads = wv // DV
    rows = heads * nq
    lb = latent.shape[1]
    nk = lb * n_ctx
    cr = C // n_dp
    cw = latent_up.shape[1] // CHUNKS
    full = C + DR
    vm = pltpu.VMEM
    dma = pltpu.SemaphoreType.DMA
    spec = pl.BlockSpec(memory_space=pltpu.VMEM)
    smem = pl.BlockSpec(memory_space=pltpu.SMEM)
    n1 = n_ctx - 1
    ys = max((ny - 1) * nz, 1)
    zs = max(nz - 1, 1)
    xs = max((nx - 1) * CHUNKS, 1)
    return pl.pallas_call(
        functools.partial(kernel, n_dp, n_ctx),
        out_shape=(
            jax.ShapeDtypeStruct(queries.shape, F32),
            jax.ShapeDtypeStruct(latent.shape, F32),
            jax.ShapeDtypeStruct((cr, latent_up.shape[1]), F32),
        ),
        in_specs=[smem, smem, spec, spec, spec, pl.BlockSpec(memory_space=pl.ANY)],
        out_specs=(spec, spec, spec),
        scratch_shapes=[
            vm(latent_up.shape, BF16),
            vm((n_ctx, rq, wq), BF16),
            vm((n_ctx, rq, wv), BF16),
            vm((nq, wq), F32),
            vm((nq, wv), F32),
            vm((heads, nq, DN), BF16),
            vm((heads, nq, DV), BF16),
            vm((rows, full), BF16),
            vm((rows, C), BF16),
            vm((n_ctx, lb, full), BF16),
            vm((rows, nk), BF16),
            vm((rows, nk), BF16),
            vm((rows, C), BF16),
            vm((rows, C), BF16),
            vm((rows, DR), F32),
            vm((CHUNKS, ncore, nx, cr, cw), BF16),
            vm((CHUNKS, nx, cr, cw), BF16),
            vm((xs, cr, cw), BF16),
            vm((xs, cr, cw), BF16),
            vm((ys, lb, full), BF16),
            vm((ys, lb, full), BF16),
            vm((nz, lb, full), F32),
            vm((zs, lb, full), BF16),
            vm((zs, lb, full), BF16),
            vm((nq, wq), F32),
            vm((n_ctx, rq, wq), F32),
            vm((n_ctx, rq, wq), F32),
            dma,
            dma((n1,)), dma((n1,)), dma((n1,)), dma((n1,)),
            dma((zs,)), dma((zs,)), dma((ys,)), dma((ys,)),
            dma((CHUNKS,)), dma((CHUNKS,)), dma((xs,)), dma((xs,)),
            dma((ys,)), dma((ys,)), dma((zs,)), dma((zs,)),
            dma((n1,)), dma((n1,)),
        ],
        compiler_params=pltpu.CompilerParams(
            collective_id=0, has_side_effects=True, vmem_limit_bytes=60 * 1024 * 1024
        ),
    )(query_start, key_lengths, queries, grad_out, latent, latent_up)


def solution(mesh):
    return jax.shard_map(
        functools.partial(local, mesh.shape["dp"], mesh.shape["ctx"]),
        mesh=mesh,
        in_specs=(
            P("dp", "ctx", None),
            P("dp", "ctx", None),
            P("dp", "ctx", None),
            P(None, "ctx"),
            P("dp"),
            P("dp"),
        ),
        out_specs=(P("dp", "ctx", None), P("dp", "ctx", None), P("dp", "ctx")),
        check_vma=False,
    )
```

time: 511 us -> 78.6 us (0.15)
  other arithmetic: 234 us -> 0 us
  local copies, waits for them, and re-layouts: 139 us -> 8.28 us
  waiting for transfers between devices: 79.4 us -> 0 us
  Pallas kernels: 0 us -> 68.1 us
  matrix products: 14.1 us -> 0 us
  starting transfers between devices: 13.6 us -> 0 us
  between operations: 15.3 us -> 1.93 us
  blocking collectives: 13.1 us -> 0 us
    unnamed x3 -> x0, other arithmetic: 227 us -> none
    unnamed x21 -> x3, local copies, waits for them, and re-layouts: 91.7 us -> 6.44 us
    pallas_call x0 -> x1, Pallas kernels: none -> 68.1 us  [local(): pl.pallas_call(functools.partial(kernel, n_dp, n_ctx), out_shape=(jax.Sha...]
    reduce_scatter x1 -> x0, waiting for transfers between devices: 44.2 us -> none  [local(): lax.psum_scatter(jnp.concatenate([key_weight, value_weight], axis=2).resh...]
    all_to_all x4 -> x0, local copies, waits for them, and re-layouts: 38.8 us -> none  [the longest x2 23.4 us: local(): lax.all_to_all(queries, 'ctx', split_axis=2, concat_axis=1, tiled=True)]
    unnamed x4 -> x0, waiting for transfers between devices: 35.1 us -> none
    dot_general x11 -> x0, matrix products: 14.1 us -> none  [the longest x1 2.25 us: local(): jnp.einsum('qhc,chd->qhd', grad_lat, w_key, preferred_element_type=jnp.fl...]
    all_to_all x2 -> x0, starting transfers between devices: 13.3 us -> none  [the longest x1 7.28 us: local(): lax.all_to_all(grad_out, 'ctx', split_axis=2, concat_axis=1, tiled=True)]
  transfers between devices with their start and end apart: 5 -> 0, of which waited for: 2 -> 0; matrix products, arithmetic and copies ran while one was open for 74% -> 0% of each run, Pallas kernels for 0% -> 0%
where the time goes in v1:
time: 78.6 us; the launch traced here: 78.4 us
  Pallas kernels  68.1 us (87%)
  local copies, waits for them, and re-layouts  8.28 us (11%)
  between operations  1.93 us (2%)
    pallas_call x1, Pallas kernels, local(): pl.pallas_call(functools.partial(kernel, n_dp, n_ctx), out_shape=(jax.Sha...  68.1 us
    unnamed x3, local copies, waits for them, and re-layouts  6.44 us
    pallas_call x1, local copies, waits for them, and re-layouts, local(): pl.pallas_call(functools.partial(kernel, n_dp, n_ctx), out_shape=(jax.Sha...  1.84 us

profile of v1, /device:TPU:0, one launch (start us, length us, event | category | flops | bytes accessed | tf_op | source)
XLA Modules:
  0.0 78.4 jit_solution(13738347591494560094)
XLA Ops:
  1.9 1.7 %copy.9.lat_ref = bf16[1,128,576]{2,1,0:T(8,128)(2,1)} copy(bf16[1,128,576]{1,2,0:T(8,128)(2,1)} %param.8) | data formatting | bytes 294912 | tf_op args[2]
  3.6 68.1 %shard_map.85 = (f32[1,2,24576]{2,1,0:T(2,128)}, f32[1,128,576]{2,1,0:T(8,128)}, f32[128,4096]{1,0:T(8,128)}) custom-call(s32[1]{0:T(128)S(6)} %copy.13.start_ref, s32[1]{0:T(128)S(6)} %copy.14.length_ref, bf16[1,2,24576]{2,1,0:T(2,128)(2,1)} %q_ref.1, bf16[1,2,16384]{2,1,0:T(2,128)(2,1)} %g_ref.1, bf16[1,128,576]{2,1,0:T(8,128)(2,1)} %copy.9.lat_ref, ...), custom_call_target="tpu_custom_call" | custom-call | tf_op jit(solution)/shard_map/pallas_call | solution.py:320
  71.8 1.8 %copy.10 = f32[1,128,576]{1,2,0:T(8,128)} copy(f32[1,128,576]{2,1,0:T(8,128)} %get-tuple-element.4) | data formatting | bytes 589824 | tf_op jit(solution)/shard_map/pallas_call | solution.py:320
  73.6 1.6 %copy.15 = f32[1,2,24576]{2,1,0:T(2,128)} copy(f32[1,2,24576]{2,1,0:T(2,128)} %get-tuple-element.9) | data formatting | bytes 393216
  75.2 3.1 %copy.16 = f32[128,4096]{1,0:T(8,128)} copy(f32[128,4096]{1,0:T(8,128)} %get-tuple-element.11) | data formatting | bytes 4194304

commit v2 on v1

v2 whole, which is shorter than its diff:
```python
import functools
import math

import jax
import jax.numpy as jnp
from jax import lax
from jax.experimental import pallas as pl
from jax.experimental.pallas import tpu as pltpu
from jax.sharding import PartitionSpec as P

DN = 128
DR = 64
DV = 128
C = 512

MSCALE = 0.1 * math.log(40.0) + 1.0
NEG_FILL = -1e30
SCALE = MSCALE * MSCALE / math.sqrt(DN + DR)
MESH = pl.DeviceIdType.MESH
F32 = jnp.float32
BF16 = jnp.bfloat16


def dot(a, b, da, db):
    return lax.dot_general(a, b, (((da,), (db,)), ((), ())), preferred_element_type=F32)


def grid_of(n):
    inner = 1
    while (2 * inner) ** 2 <= n and n % (2 * inner) == 0:
        inner *= 2
    return n // inner, inner


def kernel(
    n_dp, n_ctx, start_ref, length_ref, q_ref, g_ref, lat_ref, w_hbm,
    gq_out, gl_out, fac_out, qg_out,
    w, q_recv, g_recv, q_rows, g_rows, qg_all, q_full, g_lat, sides_t, keys,
    raw, grad_probs, low_all, grad_lat, rope_grad, fac_send, fac_all,
    kt_send, kt_recv, kt_own, z_send, z_recv, gq_rows, gq_send, gq_recv,
    w_sem, q_ss, q_rs, g_ss, g_rs, az_ss, az_rs, ay_ss, ay_rs,
    e_ss, e_rs, f_ss, f_rs, ky_ss, ky_rs, kz_ss, kz_rs, o_ss, o_rs,
):
    nz, ny = grid_of(n_ctx)
    dp = lax.axis_index("dp")
    me = lax.axis_index("ctx")
    z, y = me // ny, me % ny
    rq = q_ref.shape[1]
    nq = rq * n_ctx
    wq = q_ref.shape[2] // n_ctx
    wv = g_ref.shape[2] // n_ctx
    heads = wv // DV
    rows = heads * nq
    lb = lat_ref.shape[2]
    nk = lb * n_ctx
    cr = C // n_dp

    def ctx_dev(i):
        return (dp, i)

    def dp_dev(i):
        return (i, me)

    def copy(src, dst, ss, rs, dev):
        return pltpu.make_async_remote_copy(
            src_ref=src, dst_ref=dst, send_sem=ss, recv_sem=rs, device_id=dev, device_id_type=MESH
        )

    def cols(block):
        return pl.ds(pl.multiple_of(block * lb, lb), lb)

    w_copy = pltpu.make_async_copy(w_hbm, w, w_sem)
    w_copy.start()

    barrier = pltpu.get_barrier_semaphore()
    peers = [ctx_dev((me + d) % n_ctx) for d in range(1, n_ctx)]
    peers += [dp_dev((dp + d) % n_dp) for d in range(1, n_dp)]
    for dev in peers:
        pl.semaphore_signal(barrier, inc=1, device_id=dev, device_id_type=MESH)
    pl.semaphore_wait(barrier, len(peers))

    sends = []

    def send(*args):
        s = copy(*args)
        s.start()
        sends.append(s)

    for d in range(1, n_ctx):
        j = (me + d) % n_ctx
        at = pl.ds(pl.multiple_of(j * wq, 128), wq)
        send(q_ref.at[0, :, at], q_recv.at[me], q_ss.at[d - 1], q_rs.at[d - 1], ctx_dev(j))
        at = pl.ds(pl.multiple_of(j * wv, 128), wv)
        send(g_ref.at[0, :, at], g_recv.at[me], g_ss.at[d - 1], g_rs.at[d - 1], ctx_dev(j))

    def forward(k, src, block):
        for d in range(1, ny):
            to = z * ny + (y + d) % ny
            i = (d - 1) * nz + k
            send(src, keys.at[:, cols(block)], ay_ss.at[i], ay_rs.at[i], ctx_dev(to))

    for d in range(1, nz):
        to = ((z + d) % nz) * ny + y
        send(lat_ref.at[0], keys.at[:, cols(me)], az_ss.at[d - 1], az_rs.at[d - 1], ctx_dev(to))
    forward(0, lat_ref.at[0], me)

    def outer_in(d):
        block = ((z - d + nz) % nz) * ny + y
        ref = keys.at[:, cols(block)]
        copy(ref, ref, az_ss.at[d - 1], az_rs.at[d - 1], ctx_dev(block)).wait_recv()
        forward(d, ref, block)

    keys[:, cols(me)] = lat_ref[0]
    q_recv[me] = q_ref[0, :, pl.ds(pl.multiple_of(me * wq, 128), wq)]
    g_recv[me] = g_ref[0, :, pl.ds(pl.multiple_of(me * wv, 128), wv)]
    for d in range(1, n_ctx):
        j = (me - d + n_ctx) % n_ctx
        copy(q_recv.at[j], q_recv.at[j], q_ss.at[d - 1], q_rs.at[d - 1], ctx_dev(j)).wait_recv()
        copy(g_recv.at[j], g_recv.at[j], g_ss.at[d - 1], g_rs.at[d - 1], ctx_dev(j)).wait_recv()
    for j in range(n_ctx):
        q_rows[rq * j : rq * (j + 1), :] = q_recv[j].astype(F32)
        g_rows[rq * j : rq * (j + 1), :] = g_recv[j].astype(F32)
    w_copy.wait()

    def latents(h):
        at = slice(h * nq, (h + 1) * nq)
        qh = q_rows[:, h * (DN + DR) : (h + 1) * (DN + DR)].astype(BF16)
        gh = g_rows[:, h * DV : (h + 1) * DV].astype(BF16)
        qg_all[dp, h, :, :DN] = qh[:, :DN]
        qg_all[dp, h, :, DN:] = gh
        col = h * (DN + DV)
        q_full[at, :C] = dot(qh[:, :DN], w[:, col : col + DN], 1, 1).astype(BF16)
        q_full[at, C:] = qh[:, DN:]
        g_lat[at, :] = dot(gh, w[:, col + DN : col + DN + DV], 1, 1).astype(BF16)

    done = 1
    per = -(-heads // nz)
    for h in range(heads):
        latents(h)
        if (h + 1) % per == 0 and done < nz:
            outer_in(done)
            done += 1
    for d in range(1, n_dp):
        send(qg_all.at[dp], qg_all.at[dp], e_ss.at[d - 1], e_rs.at[d - 1], dp_dev((dp + d) % n_dp))
    for d in range(done, nz):
        outer_in(d)

    def score_block(block):
        at = cols(block)
        part = keys[:, at]
        raw[:, at] = dot(q_full[...], part, 1, 0)
        grad_probs[:, at] = dot(g_lat[...], part[:C], 1, 0)

    for k in range(nz):
        score_block(((z - k + nz) % nz) * ny + y)
    sides_t[:C, :rows] = q_full[:, :C].T
    sides_t[C:, :rows] = q_full[:, C:].T
    sides_t[:C, rows:] = g_lat[...].T
    sides_t[C:, rows:] = jnp.zeros((DR, rows), BF16)
    for k in range(nz):
        for d in range(1, ny):
            block = ((z - k + nz) % nz) * ny + (y - d + ny) % ny
            i = (d - 1) * nz + k
            ref = keys.at[:, cols(block)]
            copy(ref, ref, ay_ss.at[i], ay_rs.at[i], ctx_dev(block)).wait_recv()
            score_block(block)

    start = start_ref[0]
    low = start + nq - length_ref[0]
    rc = max(nq, 32)
    for c in range(rows // rc):
        at = slice(c * rc, (c + 1) * rc)
        key_pos = lax.broadcasted_iota(jnp.int32, (rc, nk), 1)
        row_pos = start + lax.broadcasted_iota(jnp.int32, (rc, nk), 0) % nq
        visible = (key_pos >= low) & (key_pos <= row_pos)
        masked = jnp.where(visible, raw[at, :] * SCALE, NEG_FILL)
        peak = jnp.max(masked, axis=1, keepdims=True)
        weights = jnp.where(visible, jnp.exp(masked - peak), 0.0)
        attn = weights * (1.0 / jnp.sum(weights, axis=1, keepdims=True))
        probs_low = attn.astype(BF16)
        gp = grad_probs[at, :]
        row_dot = jnp.sum(probs_low.astype(F32) * gp, axis=1, keepdims=True)
        low_all[at, :] = (SCALE * attn * (gp - row_dot)).astype(BF16)
        low_all[rows + c * rc : rows + (c + 1) * rc, :] = probs_low

    def key_block(block):
        return dot(sides_t[...], low_all[:, cols(block)], 1, 0)

    for k in range(nz):
        for d in range(1, ny):
            yi = (y + d) % ny
            i = (d - 1) * nz + k
            kt_send[i] = key_block(((z + k + 1) % nz) * ny + yi).astype(BF16)
            send(kt_send.at[i], kt_recv.at[i], ky_ss.at[i], ky_rs.at[i], ctx_dev(z * ny + yi))

    query_grad = dot(low_all[:rows, :], keys[...], 1, 1)
    rope_grad[...] = query_grad[:, C:]
    grad_lat[...] = query_grad[:, :C].astype(BF16)
    o_low = dot(low_all[rows:, :], keys[:C, :], 1, 1).astype(BF16)
    for b in range(n_dp):
        fac_send[b, :, :cr] = grad_lat[:, b * cr : (b + 1) * cr]
        fac_send[b, :, cr:] = o_low[:, b * cr : (b + 1) * cr]
    for d in range(1, n_dp):
        b = (dp + d) % n_dp
        send(fac_send.at[b], fac_all.at[dp], f_ss.at[d - 1], f_rs.at[d - 1], dp_dev(b))
    fac_all[dp] = fac_send[dp]

    def inner_sum(k):
        total = kt_own[k]
        for d in range(1, ny):
            i = (d - 1) * nz + k
            copy(kt_recv.at[i], kt_recv.at[i], ky_ss.at[i], ky_rs.at[i], ctx_dev(me)).wait_recv()
            total = total + kt_recv[i].astype(F32)
        return total

    for k in range(nz):
        kt_own[k] = key_block(((z + k + 1) % nz) * ny + y)
    for k in range(nz - 1):
        z_send[k] = inner_sum(k).astype(BF16)
        to = ((z + k + 1) % nz) * ny + y
        send(z_send.at[k], z_recv.at[k], kz_ss.at[k], kz_rs.at[k], ctx_dev(to))

    for h in range(heads):
        at = slice(h * nq, (h + 1) * nq)
        col = h * (DN + DV)
        to = h * (DN + DR)
        gq_rows[:, to : to + DN] = dot(grad_lat[at, :], w[:, col : col + DN], 1, 0)
        gq_rows[:, to + DN : to + DN + DR] = rope_grad[at, :]
    for j in range(n_ctx):
        gq_send[j] = gq_rows[rq * j : rq * (j + 1), :]
    for d in range(1, n_ctx):
        j = (me + d) % n_ctx
        send(gq_send.at[j], gq_recv.at[me], o_ss.at[d - 1], o_rs.at[d - 1], ctx_dev(j))
    gq_recv[me] = gq_send[me]

    for d in range(1, n_dp):
        b = (dp - d + n_dp) % n_dp
        copy(qg_all.at[b], qg_all.at[b], e_ss.at[d - 1], e_rs.at[d - 1], dp_dev(b)).wait_recv()
        copy(fac_all.at[b], fac_all.at[b], f_ss.at[d - 1], f_rs.at[d - 1], dp_dev(b)).wait_recv()
    qg_out[...] = qg_all[...]
    fac_out[...] = fac_all[...]

    for d in range(1, n_ctx):
        j = (me - d + n_ctx) % n_ctx
        copy(gq_recv.at[j], gq_recv.at[j], o_ss.at[d - 1], o_rs.at[d - 1], ctx_dev(j)).wait_recv()
    gq_out[...] = gq_recv[...]

    total = inner_sum(nz - 1)
    for k in range(nz - 1):
        copy(z_recv.at[k], z_recv.at[k], kz_ss.at[k], kz_rs.at[k], ctx_dev(me)).wait_recv()
        total = total + z_recv[k].astype(F32)
    gl_out[...] = total
    for s in sends:
        s.wait_send()


def finish(fac_ref, qg_ref, gq_ref, gl_ref, gq_out, gl_out, gw_out):
    n_dp, hb, nq, wide = qg_ref.shape
    cr = gw_out.shape[0]

    @pl.when(pl.program_id(0) == 0)
    def _():
        gl_out[0] = gl_ref[...]
        n_ctx, _, wq = gq_ref.shape
        for j in range(n_ctx):
            gq_out[0, :, j * wq : (j + 1) * wq] = gq_ref[j]

    for h in range(hb):
        left = fac_ref[:, h * nq : (h + 1) * nq, :].reshape(n_dp * nq, 2 * cr)
        right = qg_ref[:, h].reshape(n_dp * nq, wide)
        both = dot(left, right, 0, 0)
        at = h * wide
        gw_out[:, at : at + DN] = both[:cr, :DN]
        gw_out[:, at + DN : at + wide] = both[cr:, DN:]


def local(n_dp, n_ctx, queries, grad_out, latent, latent_up, query_start, key_lengths):
    nz, ny = grid_of(n_ctx)
    rq = queries.shape[1]
    nq = rq * n_ctx
    wq = queries.shape[2] // n_ctx
    wv = grad_out.shape[2] // n_ctx
    heads = wv // DV
    rows = heads * nq
    lb = latent.shape[1]
    nk = lb * n_ctx
    cr = C // n_dp
    full = C + DR
    wide = DN + DV
    vm = pltpu.VMEM
    dma = pltpu.SemaphoreType.DMA
    spec = pl.BlockSpec(memory_space=pltpu.VMEM)
    smem = pl.BlockSpec(memory_space=pltpu.SMEM)
    n1 = n_ctx - 1
    d1 = max(n_dp - 1, 1)
    ys = max((ny - 1) * nz, 1)
    zs = max(nz - 1, 1)
    gq, gl, fac, qg = pl.pallas_call(
        functools.partial(kernel, n_dp, n_ctx),
        out_shape=(
            jax.ShapeDtypeStruct((n_ctx, rq, wq), F32),
            jax.ShapeDtypeStruct((full, lb), F32),
            jax.ShapeDtypeStruct((n_dp, rows, 2 * cr), BF16),
            jax.ShapeDtypeStruct((n_dp, heads, nq, wide), BF16),
        ),
        in_specs=[smem, smem, spec, spec, spec, pl.BlockSpec(memory_space=pltpu.HBM)],
        out_specs=(spec, spec, spec, spec),
        scratch_shapes=[
            vm(latent_up.shape, BF16),
            vm((n_ctx, rq, wq), BF16),
            vm((n_ctx, rq, wv), BF16),
            vm((nq, wq), F32),
            vm((nq, wv), F32),
            vm((n_dp, heads, nq, wide), BF16),
            vm((rows, full), BF16),
            vm((rows, C), BF16),
            vm((full, 2 * rows), BF16),
            vm((full, nk), BF16),
            vm((rows, nk), F32),
            vm((rows, nk), F32),
            vm((2 * rows, nk), BF16),
            vm((rows, C), BF16),
            vm((rows, DR), F32),
            vm((n_dp, rows, 2 * cr), BF16),
            vm((n_dp, rows, 2 * cr), BF16),
            vm((ys, full, lb), BF16),
            vm((ys, full, lb), BF16),
            vm((nz, full, lb), F32),
            vm((zs, full, lb), BF16),
            vm((zs, full, lb), BF16),
            vm((nq, wq), F32),
            vm((n_ctx, rq, wq), F32),
            vm((n_ctx, rq, wq), F32),
            dma,
            dma((n1,)), dma((n1,)), dma((n1,)), dma((n1,)),
            dma((zs,)), dma((zs,)), dma((ys,)), dma((ys,)),
            dma((d1,)), dma((d1,)), dma((d1,)), dma((d1,)),
            dma((ys,)), dma((ys,)), dma((zs,)), dma((zs,)),
            dma((n1,)), dma((n1,)),
        ],
        compiler_params=pltpu.CompilerParams(
            collective_id=0, has_side_effects=True, vmem_limit_bytes=40 * 1024 * 1024
        ),
    )(query_start, key_lengths, queries, grad_out, jnp.swapaxes(latent, 1, 2), latent_up)
    steps = 4 if heads % 4 == 0 else 1
    hb = heads // steps

    def same(k):
        return lambda i: (0,) * k

    grad_queries, grad_latent, grad_up = pl.pallas_call(
        finish,
        grid=(steps,),
        out_shape=(
            jax.ShapeDtypeStruct(queries.shape, F32),
            jax.ShapeDtypeStruct((1, full, lb), F32),
            jax.ShapeDtypeStruct((cr, latent_up.shape[1]), F32),
        ),
        in_specs=[
            pl.BlockSpec((n_dp, hb * nq, 2 * cr), lambda i: (0, i, 0)),
            pl.BlockSpec((n_dp, hb, nq, wide), lambda i: (0, i, 0, 0)),
            pl.BlockSpec((n_ctx, rq, wq), same(3)),
            pl.BlockSpec((full, lb), same(2)),
        ],
        out_specs=(
            pl.BlockSpec(queries.shape, same(3)),
            pl.BlockSpec((1, full, lb), same(3)),
            pl.BlockSpec((cr, hb * wide), lambda i: (0, i)),
        ),
        compiler_params=pltpu.CompilerParams(vmem_limit_bytes=16 * 1024 * 1024),
    )(fac, qg, gq, gl)
    return grad_queries, jnp.swapaxes(grad_latent, 1, 2), grad_up


def solution(mesh):
    return jax.shard_map(
        functools.partial(local, mesh.shape["dp"], mesh.shape["ctx"]),
        mesh=mesh,
        in_specs=(
            P("dp", "ctx", None),
            P("dp", "ctx", None),
            P("dp", "ctx", None),
            P(None, "ctx"),
            P("dp"),
            P("dp"),
        ),
        out_specs=(P("dp", "ctx", None), P("dp", "ctx", None), P("dp", "ctx")),
        check_vma=False,
    )
```

time: 78.6 us -> 61 us (0.78)
  Pallas kernels: 68.1 us -> 53.9 us
  local copies, waits for them, and re-layouts: 8.28 us -> 4.82 us
    pallas_call x1, Pallas kernels: 68.1 us -> 51.2 us  [local(): pl.pallas_call(functools.partial(kernel, n_dp, n_ctx), out_shape=(jax.Sha...]
    pallas_call x0 -> x1, Pallas kernels: none -> 2.72 us  [local(): pl.pallas_call(finish, grid=(steps,), out_shape=(jax.ShapeDtypeStruct(que...]
    pallas_call x1 -> x0, local copies, waits for them, and re-layouts: 1.84 us -> none  [local(): pl.pallas_call(functools.partial(kernel, n_dp, n_ctx), out_shape=(jax.Sha...]
    unnamed x3 -> x8, local copies, waits for them, and re-layouts: 6.44 us -> 4.82 us
where the time goes in v2:
time: 61 us; the launch traced here: 60.7 us
  Pallas kernels  53.9 us (88%)
  local copies, waits for them, and re-layouts  4.82 us (8%)
  between operations  1.94 us (3%)
    pallas_call x1, Pallas kernels, local(): pl.pallas_call(functools.partial(kernel, n_dp, n_ctx), out_shape=(jax.Sha...  51.2 us
    unnamed x8, local copies, waits for them, and re-layouts  4.82 us
    pallas_call x1, Pallas kernels, local(): pl.pallas_call(finish, grid=(steps,), out_shape=(jax.ShapeDtypeStruct(que...  2.72 us

profile of v2, /device:TPU:0, one launch (start us, length us, event | category | flops | bytes accessed | tf_op | source)
XLA Modules:
  0.0 60.7 jit_solution(13361724903247172611)
XLA Ops:
  1.9 0.0 copy-start
  1.9 2.2 %copy-done = bf16[512,4096]{1,0:T(8,128)(2,1)S(1)} copy-done((bf16[512,4096]{1,0:T(8,128)(2,1)S(1)}, bf16[512,4096]{1,0:T(8,128)(2,1)}, u32[]{:S(2)}) %copy-start) | copy-done | bytes 4194328
  4.1 0.0 copy-start.1
  4.1 0.9 %copy-done.1 = bf16[1,128,576]{1,2,0:T(8,128)(2,1)S(1)} copy-done((bf16[1,128,576]{1,2,0:T(8,128)(2,1)S(1)}, bf16[1,128,576]{1,2,0:T(8,128)(2,1)}, u32[]{:S(2)}) %copy-start.1) | copy-done | bytes 147480
  5.0 0.0 copy-start.2
  5.0 0.9 %copy-done.2 = bf16[1,2,24576]{2,1,0:T(2,128)(2,1)S(1)} copy-done((bf16[1,2,24576]{2,1,0:T(2,128)(2,1)S(1)}, bf16[1,2,24576]{2,1,0:T(2,128)(2,1)}, u32[]{:S(2)}) %copy-start.2) | copy-done | bytes 98328
  5.9 0.0 copy-start.3
  5.9 0.8 %copy-done.3 = bf16[1,2,16384]{2,1,0:T(2,128)(2,1)S(1)} copy-done((bf16[1,2,16384]{2,1,0:T(2,128)(2,1)S(1)}, bf16[1,2,16384]{2,1,0:T(2,128)(2,1)}, u32[]{:S(2)}) %copy-start.3) | copy-done | bytes 65560
  6.8 51.2 %shard_map.85 = (f32[8,2,3072]{2,1,0:T(2,128)S(1)}, f32[576,128]{1,0:T(8,128)S(1)}, bf16[4,256,256]{2,1,0:T(8,128)(2,1)S(1)}, bf16[4,16,16,256]{3,2,1,0:T(8,128)(2,1)S(1)}) custom-call(s32[1]{0:T(128)S(6)} %copy.9.start_ref, s32[1]{0:T(128)S(6)} %copy.10.length_ref, bf16[1,2,24576]{2,1,0:T(2,128)(2,1)S(1)} %copy-done.2, bf16[1,2,16384]{2,1,0:T(2,128)(2,1)S(1)} %copy-done.3, ...), custom_call_target="tpu_custom_call" | custom-call | tf_op jit(solution)/shard_map/pallas_call | solution.py:298
  58.0 2.7 %shard_map.86 = (f32[1,2,24576]{2,1,0:T(2,128)}, f32[1,576,128]{2,1,0:T(8,128)}, f32[128,4096]{1,0:T(8,128)}) custom-call(bf16[4,256,256]{2,1,0:T(8,128)(2,1)S(1)} %get-tuple-element.10.fac_ref, bf16[4,16,16,256]{3,2,1,0:T(8,128)(2,1)S(1)} %get-tuple-element.11.qg_ref, f32[8,2,3072]{2,1,0:T(2,128)S(1)} %get-tuple-element.12.gq_ref, ...), custom_call_target="tpu_custom_call" | custom-call | tf_op jit(solution)/shard_map/pallas_call | solution.py:351
Async XLA Ops:
  1.9 2.2 %copy-start = (bf16[512,4096]{1,0:T(8,128)(2,1)S(1)}, bf16[512,4096]{1,0:T(8,128)(2,1)}, u32[]{:S(2)}) copy-start(bf16[512,4096]{1,0:T(8,128)(2,1)} %w_hbm.1) | copy-start | bytes 12582916
  4.1 0.9 %copy-start.1 = (bf16[1,128,576]{1,2,0:T(8,128)(2,1)S(1)}, bf16[1,128,576]{1,2,0:T(8,128)(2,1)}, u32[]{:S(2)}) copy-start(bf16[1,128,576]{1,2,0:T(8,128)(2,1)} %param.8) | copy-start | bytes 442372
  5.0 0.9 %copy-start.2 = (bf16[1,2,24576]{2,1,0:T(2,128)(2,1)S(1)}, bf16[1,2,24576]{2,1,0:T(2,128)(2,1)}, u32[]{:S(2)}) copy-start(bf16[1,2,24576]{2,1,0:T(2,128)(2,1)} %q_ref.1) | copy-start | bytes 294916
  5.9 0.8 %copy-start.3 = (bf16[1,2,16384]{2,1,0:T(2,128)(2,1)S(1)}, bf16[1,2,16384]{2,1,0:T(2,128)(2,1)}, u32[]{:S(2)}) copy-start(bf16[1,2,16384]{2,1,0:T(2,128)(2,1)} %g_ref.1) | copy-start | bytes 196612

commit v3 on v2

--- a/solution.py
+++ b/solution.py
@@ -38,7 +38,7 @@
     w, q_recv, g_recv, q_rows, g_rows, qg_all, q_full, g_lat, sides_t, keys,
     raw, grad_probs, low_all, grad_lat, rope_grad, fac_send, fac_all,
     kt_send, kt_recv, kt_own, z_send, z_recv, gq_rows, gq_send, gq_recv,
-    w_sem, q_ss, q_rs, g_ss, g_rs, az_ss, az_rs, ay_ss, ay_rs,
+    w_sem, own_sem, q_ss, q_rs, g_ss, g_rs, az_ss, az_rs, ay_ss, ay_rs,
     e_ss, e_rs, f_ss, f_rs, ky_ss, ky_rs, kz_ss, kz_rs, o_ss, o_rs,
 ):
     nz, ny = grid_of(n_ctx)
@@ -70,7 +70,13 @@
         return pl.ds(pl.multiple_of(block * lb, lb), lb)
 
     w_copy = pltpu.make_async_copy(w_hbm, w, w_sem)
-    w_copy.start()
+    mine = pl.ds(pl.multiple_of(me * wq, 128), wq)
+    own_q = pltpu.make_async_copy(q_ref.at[0, :, mine], q_recv.at[me], own_sem.at[0])
+    mine = pl.ds(pl.multiple_of(me * wv, 128), wv)
+    own_g = pltpu.make_async_copy(g_ref.at[0, :, mine], g_recv.at[me], own_sem.at[1])
+    own_k = pltpu.make_async_copy(lat_ref.at[0], keys.at[:, cols(me)], own_sem.at[2])
+    for own in (own_q, own_g, own_k, w_copy):
+        own.start()
 
     barrier = pltpu.get_barrier_semaphore()
     peers = [ctx_dev((me + d) % n_ctx) for d in range(1, n_ctx)]
@@ -82,9 +88,15 @@
     sends = []
 
     def send(*args):
-        s = copy(*args)
-        s.start()
-        sends.append(s)
+        copy(*args).start()
+        sends.append((None, args))
+
+    def send_if(cond, *args):
+        @pl.when(cond)
+        def _():
+            copy(*args).start()
+
+        sends.append((cond, args))
 
     for d in range(1, n_ctx):
         j = (me + d) % n_ctx
@@ -93,26 +105,52 @@
         at = pl.ds(pl.multiple_of(j * wv, 128), wv)
         send(g_ref.at[0, :, at], g_recv.at[me], g_ss.at[d - 1], g_rs.at[d - 1], ctx_dev(j))
 
-    def forward(k, src, block):
+    hops = nz - 1
+    steps = (1, -1)
+
+    def inner(k, cond, src, block):
         for d in range(1, ny):
             to = z * ny + (y + d) % ny
-            i = (d - 1) * nz + k
-            send(src, keys.at[:, cols(block)], ay_ss.at[i], ay_rs.at[i], ctx_dev(to))
-
-    for d in range(1, nz):
-        to = ((z + d) % nz) * ny + y
-        send(lat_ref.at[0], keys.at[:, cols(me)], az_ss.at[d - 1], az_rs.at[d - 1], ctx_dev(to))
-    forward(0, lat_ref.at[0], me)
-
-    def outer_in(d):
-        block = ((z - d + nz) % nz) * ny + y
-        ref = keys.at[:, cols(block)]
-        copy(ref, ref, az_ss.at[d - 1], az_rs.at[d - 1], ctx_dev(block)).wait_recv()
-        forward(d, ref, block)
-
-    keys[:, cols(me)] = lat_ref[0]
-    q_recv[me] = q_ref[0, :, pl.ds(pl.multiple_of(me * wq, 128), wq)]
-    g_recv[me] = g_ref[0, :, pl.ds(pl.multiple_of(me * wv, 128), wv)]
+            i = (d - 1) * (2 * hops + 1) + k
+            args = (src, keys.at[:, cols(block)], ay_ss.at[i], ay_rs.at[i], ctx_dev(to))
+            if cond is None:
+                send(*args)
+            else:
+                send_if(cond, *args)
+
+    def outer(line, t, has, src, block):
+        to = z + steps[line]
+        ok = has & (to >= 0) & (to < nz)
+        i = line * hops + t
+        send_if(ok, src, keys.at[:, cols(block)], az_ss.at[i], az_rs.at[i], ctx_dev(jnp.clip(to, 0, nz - 1) * ny + y))
+
+    def from_outer(line, t):
+        at = z - steps[line] * t
+        return (at >= 0) & (at < nz), jnp.clip(at, 0, nz - 1) * ny
+
+    if hops:
+        for line in range(2):
+            outer(line, 0, z >= 0, lat_ref.at[0], me)
+    inner(0, None, lat_ref.at[0], me)
+
+    def outer_in(t):
+        for line in range(2):
+            has, base = from_outer(line, t)
+            block = base + y
+            ref = keys.at[:, cols(block)]
+            i = line * hops + t - 1
+
+            @pl.when(has)
+            def _(ref=ref, i=i):
+                copy(ref, ref, az_ss.at[i], az_rs.at[i], ctx_dev(me)).wait_recv()
+
+            if t < hops:
+                outer(line, t, has, ref, block)
+            inner(1 + i, has, ref, block)
+
+    own_q.wait()
+    own_g.wait()
+    own_k.wait()
     for d in range(1, n_ctx):
         j = (me - d + n_ctx) % n_ctx
         copy(q_recv.at[j], q_recv.at[j], q_ss.at[d - 1], q_rs.at[d - 1], ctx_dev(j)).wait_recv()
@@ -157,13 +195,24 @@
     sides_t[C:, :rows] = q_full[:, C:].T
     sides_t[:C, rows:] = g_lat[...].T
     sides_t[C:, rows:] = jnp.zeros((DR, rows), BF16)
-    for k in range(nz):
-        for d in range(1, ny):
-            block = ((z - k + nz) % nz) * ny + (y - d + ny) % ny
-            i = (d - 1) * nz + k
-            ref = keys.at[:, cols(block)]
-            copy(ref, ref, ay_ss.at[i], ay_rs.at[i], ctx_dev(block)).wait_recv()
-            score_block(block)
+    for d in range(1, ny):
+        yi = (y - d + ny) % ny
+        base = (d - 1) * (2 * hops + 1)
+        ref = keys.at[:, cols(z * ny + yi)]
+        copy(ref, ref, ay_ss.at[base], ay_rs.at[base], ctx_dev(me)).wait_recv()
+        score_block(z * ny + yi)
+    for t in range(1, nz):
+        for line in range(2):
+            has, first = from_outer(line, t)
+            for d in range(1, ny):
+                block = first + (y - d + ny) % ny
+                i = (d - 1) * (2 * hops + 1) + 1 + line * hops + t - 1
+
+                @pl.when(has)
+                def _(block=block, i=i):
+                    ref = keys.at[:, cols(block)]
+                    copy(ref, ref, ay_ss.at[i], ay_rs.at[i], ctx_dev(me)).wait_recv()
+                    score_block(block)
 
     start = start_ref[0]
     low = start + nq - length_ref[0]
@@ -250,8 +299,14 @@
         copy(z_recv.at[k], z_recv.at[k], kz_ss.at[k], kz_rs.at[k], ctx_dev(me)).wait_recv()
         total = total + z_recv[k].astype(F32)
     gl_out[...] = total
-    for s in sends:
-        s.wait_send()
+    for cond, args in sends:
+        if cond is None:
+            copy(*args).wait_send()
+        else:
+
+            @pl.when(cond)
+            def _(args=args):
+                copy(*args).wait_send()
 
 
 def finish(fac_ref, qg_ref, gq_ref, gl_ref, gq_out, gl_out, gw_out):
@@ -295,6 +350,7 @@
     d1 = max(n_dp - 1, 1)
     ys = max((ny - 1) * nz, 1)
     zs = max(nz - 1, 1)
+    as_ = max((ny - 1) * (2 * nz - 1), 1)
     gq, gl, fac, qg = pl.pallas_call(
         functools.partial(kernel, n_dp, n_ctx),
         out_shape=(
@@ -303,7 +359,7 @@
             jax.ShapeDtypeStruct((n_dp, rows, 2 * cr), BF16),
             jax.ShapeDtypeStruct((n_dp, heads, nq, wide), BF16),
         ),
-        in_specs=[smem, smem, spec, spec, spec, pl.BlockSpec(memory_space=pltpu.HBM)],
+        in_specs=[smem, smem] + [pl.BlockSpec(memory_space=pltpu.HBM)] * 4,
         out_specs=(spec, spec, spec, spec),
         scratch_shapes=[
             vm(latent_up.shape, BF16),
@@ -331,9 +387,9 @@
             vm((nq, wq), F32),
             vm((n_ctx, rq, wq), F32),
             vm((n_ctx, rq, wq), F32),
-            dma,
+            dma, dma((3,)),
             dma((n1,)), dma((n1,)), dma((n1,)), dma((n1,)),
-            dma((zs,)), dma((zs,)), dma((ys,)), dma((ys,)),
+            dma((2 * zs,)), dma((2 * zs,)), dma((as_,)), dma((as_,)),
             dma((d1,)), dma((d1,)), dma((d1,)), dma((d1,)),
             dma((ys,)), dma((ys,)), dma((zs,)), dma((zs,)),
             dma((n1,)), dma((n1,)),
@@ -341,7 +397,7 @@
         compiler_params=pltpu.CompilerParams(
             collective_id=0, has_side_effects=True, vmem_limit_bytes=40 * 1024 * 1024
         ),
-    )(query_start, key_lengths, queries, grad_out, jnp.swapaxes(latent, 1, 2), latent_up)
+    )(query_start, key_lengths, *[pltpu.with_memory_space_constraint(v, pltpu.HBM) for v in (queries, grad_out, jnp.swapaxes(latent, 1, 2), latent_up)])
     steps = 4 if heads % 4 == 0 else 1
     hb = heads // steps
 

time: 61 us -> 54.2 us (0.89)
  local copies, waits for them, and re-layouts: 4.82 us -> 0 us
  Pallas kernels: 53.9 us -> 52.1 us
    unnamed x8 -> x0, local copies, waits for them, and re-layouts: 4.82 us -> none
    pallas_call x1, Pallas kernels: 51.2 us -> 49.4 us  [local(): pl.pallas_call(functools.partial(kernel, n_dp, n_ctx), out_shape=(jax.Sha...]
where the time goes in v3:
time: 54.2 us; the launch traced here: 54 us
  Pallas kernels  52.1 us (96%)
  between operations  1.93 us (4%)
    pallas_call x1, Pallas kernels, local(): pl.pallas_call(functools.partial(kernel, n_dp, n_ctx), out_shape=(jax.Sha...  49.4 us
    pallas_call x1, Pallas kernels, local(): pl.pallas_call(finish, grid=(steps,), out_shape=(jax.ShapeDtypeStruct(que...  2.72 us

profile of v3, /device:TPU:0, one launch (start us, length us, event | category | flops | bytes accessed | tf_op | source)
XLA Modules:
  0.0 54.0 jit_solution(9980210667681461852)
XLA Ops:
  1.9 49.4 %shard_map.85 = (f32[8,2,3072]{2,1,0:T(2,128)S(1)}, f32[576,128]{1,0:T(8,128)S(1)}, bf16[4,256,256]{2,1,0:T(8,128)(2,1)S(1)}, bf16[4,16,16,256]{3,2,1,0:T(8,128)(2,1)S(1)}) custom-call(s32[1]{0:T(128)S(6)} %copy.9.start_ref, s32[1]{0:T(128)S(6)} %copy.10.length_ref, bf16[1,2,24576]{2,1,0:T(2,128)(2,1)} %q_ref.1, bf16[1,2,16384]{2,1,0:T(2,128)(2,1)} %g_ref.1, ...), custom_call_target="tpu_custom_call" | custom-call | tf_op jit(solution)/shard_map/pallas_call | solution.py:354
  51.3 2.7 %shard_map.86 = (f32[1,2,24576]{2,1,0:T(2,128)}, f32[1,576,128]{2,1,0:T(8,128)}, f32[128,4096]{1,0:T(8,128)}) custom-call(bf16[4,256,256]{2,1,0:T(8,128)(2,1)S(1)} %get-tuple-element.10.fac_ref, bf16[4,16,16,256]{3,2,1,0:T(8,128)(2,1)S(1)} %get-tuple-element.11.qg_ref, f32[8,2,3072]{2,1,0:T(2,128)S(1)} %get-tuple-element.12.gq_ref, ...), custom_call_target="tpu_custom_call" | custom-call | tf_op jit(solution)/shard_map/pallas_call | solution.py:407

commit v4 on v3

--- a/solution.py
+++ b/solution.py
@@ -236,10 +236,11 @@
         return dot(sides_t[...], low_all[:, cols(block)], 1, 0)
 
     for k in range(nz):
+        slot = jnp.where((2 * z < nz) & (k < nz - 1), nz - 2 - k, k)
         for d in range(1, ny):
             yi = (y + d) % ny
-            i = (d - 1) * nz + k
-            kt_send[i] = key_block(((z + k + 1) % nz) * ny + yi).astype(BF16)
+            i = (d - 1) * nz + slot
+            kt_send[i] = key_block(((z + slot + 1) % nz) * ny + yi).astype(BF16)
             send(kt_send.at[i], kt_recv.at[i], ky_ss.at[i], ky_rs.at[i], ctx_dev(z * ny + yi))
 
     query_grad = dot(low_all[:rows, :], keys[...], 1, 1)
@@ -264,10 +265,30 @@
 
     for k in range(nz):
         kt_own[k] = key_block(((z + k + 1) % nz) * ny + y)
-    for k in range(nz - 1):
-        z_send[k] = inner_sum(k).astype(BF16)
-        to = ((z + k + 1) % nz) * ny + y
-        send(z_send.at[k], z_recv.at[k], kz_ss.at[k], kz_rs.at[k], ctx_dev(to))
+    for t in range(hops, 0, -1):
+        for line in range(2):
+            owner = z + steps[line] * t
+            prev = z - steps[line]
+            ok = (owner >= 0) & (owner < nz)
+            i = line * hops + t - 1
+
+            @pl.when(ok)
+            def _(k=t - 1 if line == 0 else hops - t, i=i):
+                kt_own[k] = inner_sum(k)
+
+            if t < hops:
+
+                @pl.when(ok & (prev >= 0) & (prev < nz))
+                def _(k=t - 1 if line == 0 else hops - t, i=i):
+                    copy(z_recv.at[i + 1], z_recv.at[i + 1], kz_ss.at[i + 1], kz_rs.at[i + 1], ctx_dev(me)).wait_recv()
+                    kt_own[k] = kt_own[k] + z_recv[i + 1].astype(F32)
+
+            @pl.when(ok)
+            def _(k=t - 1 if line == 0 else hops - t, i=i):
+                z_send[i] = kt_own[k].astype(BF16)
+
+            to = jnp.clip(z + steps[line], 0, nz - 1) * ny + y
+            send_if(ok, z_send.at[i], z_recv.at[i], kz_ss.at[i], kz_rs.at[i], ctx_dev(to))
 
     for h in range(heads):
         at = slice(h * nq, (h + 1) * nq)
@@ -294,11 +315,16 @@
         copy(gq_recv.at[j], gq_recv.at[j], o_ss.at[d - 1], o_rs.at[d - 1], ctx_dev(j)).wait_recv()
     gq_out[...] = gq_recv[...]
 
-    total = inner_sum(nz - 1)
-    for k in range(nz - 1):
-        copy(z_recv.at[k], z_recv.at[k], kz_ss.at[k], kz_rs.at[k], ctx_dev(me)).wait_recv()
-        total = total + z_recv[k].astype(F32)
-    gl_out[...] = total
+    gl_out[...] = inner_sum(nz - 1)
+    if hops:
+        for line in range(2):
+            prev = z - steps[line]
+
+            @pl.when((prev >= 0) & (prev < nz))
+            def _(i=line * hops):
+                copy(z_recv.at[i], z_recv.at[i], kz_ss.at[i], kz_rs.at[i], ctx_dev(me)).wait_recv()
+                gl_out[...] = gl_out[...] + z_recv[i].astype(F32)
+
     for cond, args in sends:
         if cond is None:
             copy(*args).wait_send()
@@ -382,8 +408,8 @@
             vm((ys, full, lb), BF16),
             vm((ys, full, lb), BF16),
             vm((nz, full, lb), F32),
-            vm((zs, full, lb), BF16),
-            vm((zs, full, lb), BF16),
+            vm((2 * zs, full, lb), BF16),
+            vm((2 * zs, full, lb), BF16),
             vm((nq, wq), F32),
             vm((n_ctx, rq, wq), F32),
             vm((n_ctx, rq, wq), F32),
@@ -391,11 +417,11 @@
             dma((n1,)), dma((n1,)), dma((n1,)), dma((n1,)),
             dma((2 * zs,)), dma((2 * zs,)), dma((as_,)), dma((as_,)),
             dma((d1,)), dma((d1,)), dma((d1,)), dma((d1,)),
-            dma((ys,)), dma((ys,)), dma((zs,)), dma((zs,)),
+            dma((ys,)), dma((ys,)), dma((2 * zs,)), dma((2 * zs,)),
             dma((n1,)), dma((n1,)),
         ],
         compiler_params=pltpu.CompilerParams(
-            collective_id=0, has_side_effects=True, vmem_limit_bytes=40 * 1024 * 1024
+            collective_id=0, has_side_effects=True, vmem_limit_bytes=48 * 1024 * 1024
         ),
     )(query_start, key_lengths, *[pltpu.with_memory_space_constraint(v, pltpu.HBM) for v in (queries, grad_out, jnp.swapaxes(latent, 1, 2), latent_up)])
     steps = 4 if heads % 4 == 0 else 1

time: 54.2 us -> 55 us (1.015)
  Pallas kernels: 52.1 us -> 52.9 us
    pallas_call x1, Pallas kernels: 49.4 us -> 50.1 us  [local(): pl.pallas_call(functools.partial(kernel, n_dp, n_ctx), out_shape=(jax.Sha...]
where the time goes in v4:
time: 55 us; the launch traced here: 54.8 us
  Pallas kernels  52.9 us (96%)
  between operations  1.93 us (4%)
    pallas_call x1, Pallas kernels, local(): pl.pallas_call(functools.partial(kernel, n_dp, n_ctx), out_shape=(jax.Sha...  50.1 us
    pallas_call x1, Pallas kernels, local(): pl.pallas_call(finish, grid=(steps,), out_shape=(jax.ShapeDtypeStruct(que...  2.73 us

profile of v4, /device:TPU:0, one launch (start us, length us, event | category | flops | bytes accessed | tf_op | source)
XLA Modules:
  0.0 54.8 jit_solution(14089912030347882254)
XLA Ops:
  1.9 50.1 %shard_map.85 = (f32[8,2,3072]{2,1,0:T(2,128)S(1)}, f32[576,128]{1,0:T(8,128)S(1)}, bf16[4,256,256]{2,1,0:T(8,128)(2,1)S(1)}, bf16[4,16,16,256]{3,2,1,0:T(8,128)(2,1)S(1)}) custom-call(s32[1]{0:T(128)S(6)} %copy.9.start_ref, s32[1]{0:T(128)S(6)} %copy.10.length_ref, bf16[1,2,24576]{2,1,0:T(2,128)(2,1)} %q_ref.1, bf16[1,2,16384]{2,1,0:T(2,128)(2,1)} %g_ref.1, ...), custom_call_target="tpu_custom_call" | custom-call | tf_op jit(solution)/shard_map/pallas_call | solution.py:380
  52.1 2.7 %shard_map.86 = (f32[1,2,24576]{2,1,0:T(2,128)}, f32[1,576,128]{2,1,0:T(8,128)}, f32[128,4096]{1,0:T(8,128)}) custom-call(bf16[4,256,256]{2,1,0:T(8,128)(2,1)S(1)} %get-tuple-element.10.fac_ref, bf16[4,16,16,256]{3,2,1,0:T(8,128)(2,1)S(1)} %get-tuple-element.11.qg_ref, f32[8,2,3072]{2,1,0:T(2,128)S(1)} %get-tuple-element.12.gq_ref, ...), custom_call_target="tpu_custom_call" | custom-call | tf_op jit(solution)/shard_map/pallas_call | solution.py:433
